TPU v7x, 256 devices: a whole 4x4x8 slice. The times are simulated.
256 devices in a mesh: rows: 64 (over y, z, core), rhs: 4 (over x).
Axes of the slice: x: 4, y: 4, z: 8, core: 2. Of those that a mesh axis runs over, the one named last changes fastest.
Arguments:
- right_side: bfloat16 [512, 512, 256], P('rows', 'rhs'), may hold values from -6 to 6
- off_blocks: bfloat16 [512, 8, 256, 256], P('rows', None, 'rhs'), may hold values from -0.125 to 0.125
- diag_inverse: bfloat16 [512, 256, 256], P('rows', 'rhs'), may hold values from -0.375 to 0.375
- block_level: int32 [512], P('rows'), may hold values from 0 to 3, as said below
- block_columns: int32 [512, 8], P('rows'), may hold values from 0 to 511, as said below
Outputs:
- solved: bfloat16 [512, 512, 256], P('rows', 'rhs')
Inputs may be any that keep to these rules, and one draw needn't show every extreme that they name: `block_level`: among the 8 block rows of one index of rows every level occurs, none more than 4 times, and one level exactly 4 times. `block_columns`: block row i lies on index i // 8 of rows; each of its 8 block columns is a block row on the same index or one of the 3 indices below it (none below 0), of lower level when block row i has level 1 or more. Columns of one block row may repeat.
All inputs are finite; a program needn't handle non-finite values.
Results may differ from a plain program's by a relative error of at most 0.0075.
Values may be sent and summed in bfloat16 or wider, within the bound.
No kernel may reach another device: no remote copies, remote signals or barrier semaphores. Data moves between devices by JAX's collectives and lax.ppermute only.
A program may use at most 128 MiB of HBM per device.

v0:
```python
import jax
import jax.numpy as jnp
from jax import lax
from jax.sharding import PartitionSpec as P

LEVELS = 4
REACH = 4


def shifted(block, axis, distance):
    devices = range(lax.axis_size(axis))
    route = [(i - distance, i) for i in devices if i - distance in devices]
    return lax.ppermute(block, axis, route)


def per_device(right_side, off_blocks, diag_inverse, block_level, block_columns):
    full_off, full_diag = (
        lax.all_gather(off_blocks, "rhs", axis=2, tiled=True),
        lax.all_gather(diag_inverse, "rhs", axis=1, tiled=True),
    )
    rows_here = block_level.shape[0]
    anchor = lax.axis_index("rows") * rows_here
    picked = jnp.zeros((rows_here, block_columns.shape[1]) + right_side.shape[1:], jnp.bfloat16)
    solved = jnp.zeros_like(right_side)
    source = right_side.astype(jnp.float32)
    for level_now in range(LEVELS):
        if level_now > 0:
            pieces = [solved]
            for distance in range(1, REACH):
                pieces.insert(0, shifted(solved, "rows", distance))
            window = jnp.concatenate(pieces, axis=0)
            begin_at = anchor - (REACH - 1) * rows_here
            offset = jnp.clip(block_columns - begin_at, 0, window.shape[0] - 1)
            picked = jnp.take(window, offset, axis=0)
            contribution = jnp.einsum(
                "ikrb,ikab->ira", picked, full_off, preferred_element_type=jnp.float32
            )
            residue = (source - contribution).astype(jnp.bfloat16)
        else:
            residue = right_side
        updated = jnp.einsum("irb,iab->ira", residue, full_diag, preferred_element_type=jnp.float32)
        solved = jnp.where(
            (block_level == level_now)[:, None, None], updated.astype(jnp.bfloat16), solved
        )
    return solved


def solution(mesh):
    return jax.shard_map(
        per_device,
        mesh=mesh,
        in_specs=(
            P("rows", "rhs", None),
            P("rows", None, "rhs", None),
            P("rows", "rhs", None),
            P("rows"),
            P("rows", None),
        ),
        out_specs=P("rows", "rhs", None),
        check_vma=False,
    )
```

profile of v0, /device:TPU:8, one launch (start us, length us, event | category | flops | bytes accessed | tf_op | source)
XLA Modules:
  0.0 244.2 jit_solution(7970697791288904831)
XLA Ops:
  6.5 0.0 copy-start.5
  6.5 0.0 all-gather.3.cloned.1.call-start
  6.5 0.7 all-gather.3.cloned.1.call-update
  7.3 0.0 all-gather.5.cloned.1.call-start
  7.3 0.7 all-gather.5.cloned.1.call-update
  8.0 0.7 broadcast_compare_fusion.3
  8.7 29.9 %all-gather.3.cloned.1.call-done = bf16[8,256,256]{2,1,0:T(8,128)(2,1)} async-done(((bf16[8,64,256]{2,1,0:T(8,128)(2,1)}), bf16[8,256,256]{2,1,0:T(8,128)(2,1)}) %all-gather.3.cloned.1.call-update) | async-done | bytes 1048592 | tf_op jit(solution)/shard_map/all_gather | solution.py:19
  38.6 1.9 fusion.36
  40.4 2.0 collective-permute-start
  42.5 3.5 %collective-permute-start.1 = (bf16[8,128,256]{2,1,0:T(8,128)(2,1)S(1)}, bf16[8,128,256]{2,1,0:T(8,128)(2,1)S(1)}, u32[]{:S(2)}, u32[]{:S(2)}) collective-permute-start(bf16[8,128,256]{2,1,0:T(8,128)(2,1)S(1)} %fusion.36), channel_id=1, source_target_pairs={{0,8},{4,12},{8,16},{12,20},{16,24},{20,28},{24,32},{28,36},{32,40... | collective-permute-start | bytes 1572872 | tf_op jit(solution)/shard_map/ppermute | solution.py:13
  45.9 4.2 %collective-permute-start.2 = (bf16[8,128,256]{2,1,0:T(8,128)(2,1)S(1)}, bf16[8,128,256]{2,1,0:T(8,128)(2,1)}, u32[]{:S(2)}, u32[]{:S(2)}) collective-permute-start(bf16[8,128,256]{2,1,0:T(8,128)(2,1)S(1)} %fusion.36), channel_id=1, source_target_pairs={{0,4},{4,8},{8,12},{12,16},{16,20},{20,24},{24,28},{28,32},{32,36}... | collective-permute-start | bytes 1572872 | tf_op jit(solution)/shard_map/ppermute | solution.py:13
  50.1 0.0 copy-done.5
  50.2 0.1 reshape.39
  50.3 14.5 %collective-permute-done = bf16[8,128,256]{2,1,0:T(8,128)(2,1)S(1)} collective-permute-done((bf16[8,128,256]{2,1,0:T(8,128)(2,1)S(1)}, bf16[8,128,256]{2,1,0:T(8,128)(2,1)S(1)}, u32[]{:S(2)}, u32[]{:S(2)}) %collective-permute-start) | collective-permute-done | bytes 524320 | tf_op jit(solution)/shard_map/ppermute | solution.py:13
  64.7 9.3 %collective-permute-done.1 = bf16[8,128,256]{2,1,0:T(8,128)(2,1)S(1)} collective-permute-done((bf16[8,128,256]{2,1,0:T(8,128)(2,1)S(1)}, bf16[8,128,256]{2,1,0:T(8,128)(2,1)S(1)}, u32[]{:S(2)}, u32[]{:S(2)}) %collective-permute-start.1) | collective-permute-done | bytes 524320 | tf_op jit(solution)/shard_map/ppermute | solution.py:13
  74.0 0.0 copy-start.2
  74.0 0.8 copy-done.2
  74.8 6.2 %collective-permute-done.2 = bf16[8,128,256]{2,1,0:T(8,128)(2,1)} collective-permute-done((bf16[8,128,256]{2,1,0:T(8,128)(2,1)S(1)}, bf16[8,128,256]{2,1,0:T(8,128)(2,1)}, u32[]{:S(2)}, u32[]{:S(2)}) %collective-permute-start.2) | collective-permute-done | bytes 524320 | tf_op jit(solution)/shard_map/ppermute | solution.py:13
  81.0 1.5 pad_maximum_fusion
  82.5 0.0 copy-start.1
  82.5 2.8 %gather_fusion = bf16[64,128,256]{2,1,0:T(8,128)(2,1)} fusion(bf16[32,128,256]{2,1,0:T(8,128)(2,1)S(1)} %pad_maximum_fusion, s32[1024]{0:T(1024)S(1)} %pad_clamp_fusion), kind=kCustom, calls=%fused_computation.clone | custom fusion | bytes 8388864 | tf_op jit(solution)/shard_map/jit(_take)/gather | solution.py:34
  85.3 41.2 %all-gather.5.cloned.1.call-done = bf16[8,8,256,256]{3,2,1,0:T(8,128)(2,1)} async-done(((bf16[8,8,64,256]{3,2,1,0:T(8,128)(2,1)}), bf16[8,8,256,256]{3,2,1,0:T(8,128)(2,1)}) %all-gather.5.cloned.1.call-update) | async-done | bytes 8388624 | tf_op jit(solution)/shard_map/all_gather | solution.py:18
  126.4 0.0 copy-done.1
  126.4 8.0 %fusion.37 = bf16[8,128,256]{2,1,0:T(8,128)(2,1)S(1)} fusion(bf16[8,128,256]{2,1,0:T(8,128)(2,1)S(1)} %fusion.36, bf16[8,256,256]{2,1,0:T(8,128)(2,1)} %all-gather.3.cloned.1.call-done, bf16[8,8,256,256]{3,2,1,0:T(8,128)(2,1)} %all-gather.5.cloned.1.call-done, bf16[8,8,128,256]{3,2,1,0:T(8,128)(2,1)} %bitcast.39, pred[8,8]{1,0:T(8,128)(4,1)S(1)} %get-tuple-element.6, ...), kind=kOutput, calls=%fused_computation.32 | convolution fusion | flops 1211367424 | bytes 15204424 | tf_op jit(solution)/shard_map/irb,iab->ira/dot_general | solution.py:41
  134.4 0.0 copy-start.4
  134.4 2.9 %collective-permute-start.3 = (bf16[8,128,256]{2,1,0:T(8,128)(2,1)S(1)}, bf16[8,128,256]{2,1,0:T(8,128)(2,1)S(1)}, u32[]{:S(2)}, u32[]{:S(2)}) collective-permute-start(bf16[8,128,256]{2,1,0:T(8,128)(2,1)S(1)} %fusion.37), channel_id=1, source_target_pairs={{0,12},{4,16},{8,20},{12,24},{16,28},{20,32},{24,36},{28,40},{32,4... | collective-permute-start | bytes 1572872 | tf_op jit(solution)/shard_map/ppermute | solution.py:13
  137.3 3.5 %collective-permute-start.4 = (bf16[8,128,256]{2,1,0:T(8,128)(2,1)S(1)}, bf16[8,128,256]{2,1,0:T(8,128)(2,1)S(1)}, u32[]{:S(2)}, u32[]{:S(2)}) collective-permute-start(bf16[8,128,256]{2,1,0:T(8,128)(2,1)S(1)} %fusion.37), channel_id=1, source_target_pairs={{0,8},{4,12},{8,16},{12,20},{16,24},{20,28},{24,32},{28,36},{32,40... | collective-permute-start | bytes 1572872 | tf_op jit(solution)/shard_map/ppermute | solution.py:13
  140.8 3.3 %collective-permute-start.5 = (bf16[8,128,256]{2,1,0:T(8,128)(2,1)S(1)}, bf16[8,128,256]{2,1,0:T(8,128)(2,1)S(1)}, u32[]{:S(2)}, u32[]{:S(2)}) collective-permute-start(bf16[8,128,256]{2,1,0:T(8,128)(2,1)S(1)} %fusion.37), channel_id=1, source_target_pairs={{0,4},{4,8},{8,12},{12,16},{16,20},{20,24},{24,28},{28,32},{32,36}... | collective-permute-start | bytes 1572872 | tf_op jit(solution)/shard_map/ppermute | solution.py:13
  144.1 14.7 %collective-permute-done.3 = bf16[8,128,256]{2,1,0:T(8,128)(2,1)S(1)} collective-permute-done((bf16[8,128,256]{2,1,0:T(8,128)(2,1)S(1)}, bf16[8,128,256]{2,1,0:T(8,128)(2,1)S(1)}, u32[]{:S(2)}, u32[]{:S(2)}) %collective-permute-start.3) | collective-permute-done | bytes 524320 | tf_op jit(solution)/shard_map/ppermute | solution.py:13
  158.9 9.6 %collective-permute-done.4 = bf16[8,128,256]{2,1,0:T(8,128)(2,1)S(1)} collective-permute-done((bf16[8,128,256]{2,1,0:T(8,128)(2,1)S(1)}, bf16[8,128,256]{2,1,0:T(8,128)(2,1)S(1)}, u32[]{:S(2)}, u32[]{:S(2)}) %collective-permute-start.4) | collective-permute-done | bytes 524320 | tf_op jit(solution)/shard_map/ppermute | solution.py:13
  168.5 6.6 %collective-permute-done.5 = bf16[8,128,256]{2,1,0:T(8,128)(2,1)S(1)} collective-permute-done((bf16[8,128,256]{2,1,0:T(8,128)(2,1)S(1)}, bf16[8,128,256]{2,1,0:T(8,128)(2,1)S(1)}, u32[]{:S(2)}, u32[]{:S(2)}) %collective-permute-start.5) | collective-permute-done | bytes 524320 | tf_op jit(solution)/shard_map/ppermute | solution.py:13
  175.1 0.0 copy-done.4
  175.1 0.3 pad_maximum_fusion.1
  175.4 0.0 copy-start
  175.4 2.8 %gather_fusion.1 = bf16[64,128,256]{2,1,0:T(8,128)(2,1)} fusion(bf16[32,128,256]{2,1,0:T(8,128)(2,1)S(1)} %pad_maximum_fusion.1, s32[1024]{0:T(1024)S(1)} %pad_clamp_fusion), kind=kCustom, calls=%fused_computation.1.clone | custom fusion | bytes 8388864 | tf_op jit(solution)/shard_map/jit(_take)/gather | solution.py:34
  178.2 0.0 copy-done
  178.2 8.0 %fusion.38 = bf16[8,128,256]{2,1,0:T(8,128)(2,1)S(1)} fusion(bf16[8,128,256]{2,1,0:T(8,128)(2,1)} %copy-done.4, bf16[8,256,256]{2,1,0:T(8,128)(2,1)S(1)} %copy-done, bf16[8,8,256,256]{3,2,1,0:T(8,128)(2,1)} %all-gather.5.cloned.1.call-done, bf16[8,8,128,256]{3,2,1,0:T(8,128)(2,1)} %bitcast.40, pred[8,8]{1,0:T(8,128)(4,1)S(1)} %get-tuple-element.6, ...), kind=kOutput, calls=%fused_computation.33 | convolution fusion | flops 1211367424 | bytes 15204424 | tf_op jit(solution)/shard_map/irb,iab->ira/dot_general | solution.py:41
  186.1 0.0 copy-start.3
  186.2 1.9 collective-permute-start.6
  188.1 1.9 collective-permute-start.7
  190.0 3.7 %collective-permute-start.8 = (bf16[8,128,256]{2,1,0:T(8,128)(2,1)S(1)}, bf16[8,128,256]{2,1,0:T(8,128)(2,1)S(1)}, u32[]{:S(2)}, u32[]{:S(2)}) collective-permute-start(bf16[8,128,256]{2,1,0:T(8,128)(2,1)S(1)} %fusion.38), channel_id=1, source_target_pairs={{0,4},{4,8},{8,12},{12,16},{16,20},{20,24},{24,28},{28,32},{32,36}... | collective-permute-start | bytes 1572872 | tf_op jit(solution)/shard_map/ppermute | solution.py:13
  193.7 16.8 %collective-permute-done.6 = bf16[8,128,256]{2,1,0:T(8,128)(2,1)S(1)} collective-permute-done((bf16[8,128,256]{2,1,0:T(8,128)(2,1)S(1)}, bf16[8,128,256]{2,1,0:T(8,128)(2,1)S(1)}, u32[]{:S(2)}, u32[]{:S(2)}) %collective-permute-start.6) | collective-permute-done | bytes 524320 | tf_op jit(solution)/shard_map/ppermute | solution.py:13
  210.5 7.1 %collective-permute-done.7 = bf16[8,128,256]{2,1,0:T(8,128)(2,1)S(1)} collective-permute-done((bf16[8,128,256]{2,1,0:T(8,128)(2,1)S(1)}, bf16[8,128,256]{2,1,0:T(8,128)(2,1)S(1)}, u32[]{:S(2)}, u32[]{:S(2)}) %collective-permute-start.7) | collective-permute-done | bytes 524320 | tf_op jit(solution)/shard_map/ppermute | solution.py:13
  217.6 0.0 copy-done.3
  217.6 6.9 %collective-permute-done.8 = bf16[8,128,256]{2,1,0:T(8,128)(2,1)S(1)} collective-permute-done((bf16[8,128,256]{2,1,0:T(8,128)(2,1)S(1)}, bf16[8,128,256]{2,1,0:T(8,128)(2,1)S(1)}, u32[]{:S(2)}, u32[]{:S(2)}) %collective-permute-start.8) | collective-permute-done | bytes 524320 | tf_op jit(solution)/shard_map/ppermute | solution.py:13
  224.5 1.3 pad_maximum_fusion.2
  225.8 2.8 %gather_fusion.2 = bf16[64,128,256]{2,1,0:T(8,128)(2,1)} fusion(bf16[32,128,256]{2,1,0:T(8,128)(2,1)S(1)} %pad_maximum_fusion.2, s32[1024]{0:T(1024)S(1)} %pad_clamp_fusion), kind=kCustom, calls=%fused_computation.2.clone | custom fusion | bytes 8388864 | tf_op jit(solution)/shard_map/jit(_take)/gather | solution.py:34
  228.6 8.7 %fusion.39 = bf16[8,128,256]{2,1,0:T(8,128)(2,1)} fusion(bf16[8,128,256]{2,1,0:T(8,128)(2,1)} %copy-done.3, bf16[8,256,256]{2,1,0:T(8,128)(2,1)S(1)} %copy-done, bf16[8,8,256,256]{3,2,1,0:T(8,128)(2,1)} %all-gather.5.cloned.1.call-done, bf16[8,8,128,256]{3,2,1,0:T(8,128)(2,1)} %bitcast.38, pred[8,8]{1,0:T(8,128)(4,1)S(1)} %get-tuple-element.6, ...), kind=kOutput, calls=%fused_computation.34 | convolution fusion | flops 1211367424 | bytes 15204424 | tf_op jit(solution)/shard_map/irb,iab->ira/dot_general | solution.py:41
  (2 shorter events, 0.0 us)
Async XLA Ops:
  6.5 43.6 %copy-start.5 = (s32[8,8]{1,0:T(8,128)S(1)}, s32[8,8]{1,0:T(8,128)}, u32[]{:S(2)}) copy-start(s32[8,8]{1,0:T(8,128)} %param.11) | copy-start | bytes 772
  6.5 32.0 %all-gather.3.cloned.1.call-start = ((), (), s32[]{:S(2)}) async-start(), calls=%async_computation | async-start | bytes 1310720 | tf_op jit(solution)/shard_map/all_gather | solution.py:19
  7.3 119.2 %all-gather.5.cloned.1.call-start = ((), (), s32[]{:S(2)}) async-start(), calls=%async_computation.1 | async-start | bytes 10485760 | tf_op jit(solution)/shard_map/all_gather | solution.py:18
  40.4 24.3 %collective-permute-start = (bf16[8,128,256]{2,1,0:T(8,128)(2,1)S(1)}, bf16[8,128,256]{2,1,0:T(8,128)(2,1)S(1)}, u32[]{:S(2)}, u32[]{:S(2)}) collective-permute-start(bf16[8,128,256]{2,1,0:T(8,128)(2,1)S(1)} %fusion.36), channel_id=1, source_target_pairs={{0,12},{4,16},{8,20},{12,24},{16,28},{20,32},{24,36},{28,40},{32,4... | collective-permute-start | bytes 1572872 | tf_op jit(solution)/shard_map/ppermute | solution.py:13
  42.5 31.5 %collective-permute-start.1 = (bf16[8,128,256]{2,1,0:T(8,128)(2,1)S(1)}, bf16[8,128,256]{2,1,0:T(8,128)(2,1)S(1)}, u32[]{:S(2)}, u32[]{:S(2)}) collective-permute-start(bf16[8,128,256]{2,1,0:T(8,128)(2,1)S(1)} %fusion.36), channel_id=1, source_target_pairs={{0,8},{4,12},{8,16},{12,20},{16,24},{20,28},{24,32},{28,36},{32,40... | collective-permute-start | bytes 1572872 | tf_op jit(solution)/shard_map/ppermute | solution.py:13
  45.9 35.1 %collective-permute-start.2 = (bf16[8,128,256]{2,1,0:T(8,128)(2,1)S(1)}, bf16[8,128,256]{2,1,0:T(8,128)(2,1)}, u32[]{:S(2)}, u32[]{:S(2)}) collective-permute-start(bf16[8,128,256]{2,1,0:T(8,128)(2,1)S(1)} %fusion.36), channel_id=1, source_target_pairs={{0,4},{4,8},{8,12},{12,16},{16,20},{20,24},{24,28},{28,32},{32,36}... | collective-permute-start | bytes 1572872 | tf_op jit(solution)/shard_map/ppermute | solution.py:13
  74.0 0.8 copy-start.2
  82.5 44.0 %copy-start.1 = (bf16[8,128,256]{2,1,0:T(8,128)(2,1)S(1)}, bf16[8,128,256]{2,1,0:T(8,128)(2,1)}, u32[]{:S(2)}) copy-start(bf16[8,128,256]{2,1,0:T(8,128)(2,1)} %param.7) | copy-start | bytes 1572868
  134.4 40.7 %copy-start.4 = (bf16[8,128,256]{2,1,0:T(8,128)(2,1)}, bf16[8,128,256]{2,1,0:T(8,128)(2,1)S(1)}, u32[]{:S(2)}) copy-start(bf16[8,128,256]{2,1,0:T(8,128)(2,1)S(1)} %fusion.37) | copy-start | bytes 1572868
  134.4 24.4 %collective-permute-start.3 = (bf16[8,128,256]{2,1,0:T(8,128)(2,1)S(1)}, bf16[8,128,256]{2,1,0:T(8,128)(2,1)S(1)}, u32[]{:S(2)}, u32[]{:S(2)}) collective-permute-start(bf16[8,128,256]{2,1,0:T(8,128)(2,1)S(1)} %fusion.37), channel_id=1, source_target_pairs={{0,12},{4,16},{8,20},{12,24},{16,28},{20,32},{24,36},{28,40},{32,4... | collective-permute-start | bytes 1572872 | tf_op jit(solution)/shard_map/ppermute | solution.py:13
  137.3 31.2 %collective-permute-start.4 = (bf16[8,128,256]{2,1,0:T(8,128)(2,1)S(1)}, bf16[8,128,256]{2,1,0:T(8,128)(2,1)S(1)}, u32[]{:S(2)}, u32[]{:S(2)}) collective-permute-start(bf16[8,128,256]{2,1,0:T(8,128)(2,1)S(1)} %fusion.37), channel_id=1, source_target_pairs={{0,8},{4,12},{8,16},{12,20},{16,24},{20,28},{24,32},{28,36},{32,40... | collective-permute-start | bytes 1572872 | tf_op jit(solution)/shard_map/ppermute | solution.py:13
  140.8 34.3 %collective-permute-start.5 = (bf16[8,128,256]{2,1,0:T(8,128)(2,1)S(1)}, bf16[8,128,256]{2,1,0:T(8,128)(2,1)S(1)}, u32[]{:S(2)}, u32[]{:S(2)}) collective-permute-start(bf16[8,128,256]{2,1,0:T(8,128)(2,1)S(1)} %fusion.37), channel_id=1, source_target_pairs={{0,4},{4,8},{8,12},{12,16},{16,20},{20,24},{24,28},{28,32},{32,36}... | collective-permute-start | bytes 1572872 | tf_op jit(solution)/shard_map/ppermute | solution.py:13
  175.4 2.8 %copy-start = (bf16[8,256,256]{2,1,0:T(8,128)(2,1)S(1)}, bf16[8,256,256]{2,1,0:T(8,128)(2,1)}, u32[]{:S(2)}) copy-start(bf16[8,256,256]{2,1,0:T(8,128)(2,1)} %all-gather.3.cloned.1.call-done) | copy-start | bytes 3145732
  186.1 31.5 %copy-start.3 = (bf16[8,128,256]{2,1,0:T(8,128)(2,1)}, bf16[8,128,256]{2,1,0:T(8,128)(2,1)S(1)}, u32[]{:S(2)}) copy-start(bf16[8,128,256]{2,1,0:T(8,128)(2,1)S(1)} %fusion.38) | copy-start | bytes 1572868
  186.2 24.4 %collective-permute-start.6 = (bf16[8,128,256]{2,1,0:T(8,128)(2,1)S(1)}, bf16[8,128,256]{2,1,0:T(8,128)(2,1)S(1)}, u32[]{:S(2)}, u32[]{:S(2)}) collective-permute-start(bf16[8,128,256]{2,1,0:T(8,128)(2,1)S(1)} %fusion.38), channel_id=1, source_target_pairs={{0,12},{4,16},{8,20},{12,24},{16,28},{20,32},{24,36},{28,40},{32,4... | collective-permute-start | bytes 1572872 | tf_op jit(solution)/shard_map/ppermute | solution.py:13
  188.1 29.5 %collective-permute-start.7 = (bf16[8,128,256]{2,1,0:T(8,128)(2,1)S(1)}, bf16[8,128,256]{2,1,0:T(8,128)(2,1)S(1)}, u32[]{:S(2)}, u32[]{:S(2)}) collective-permute-start(bf16[8,128,256]{2,1,0:T(8,128)(2,1)S(1)} %fusion.38), channel_id=1, source_target_pairs={{0,8},{4,12},{8,16},{12,20},{16,24},{20,28},{24,32},{28,36},{32,40... | collective-permute-start | bytes 1572872 | tf_op jit(solution)/shard_map/ppermute | solution.py:13
  190.0 34.5 %collective-permute-start.8 = (bf16[8,128,256]{2,1,0:T(8,128)(2,1)S(1)}, bf16[8,128,256]{2,1,0:T(8,128)(2,1)S(1)}, u32[]{:S(2)}, u32[]{:S(2)}) collective-permute-start(bf16[8,128,256]{2,1,0:T(8,128)(2,1)S(1)} %fusion.38), channel_id=1, source_target_pairs={{0,4},{4,8},{8,12},{12,16},{16,20},{20,24},{24,28},{28,32},{32,36}... | collective-permute-start | bytes 1572872 | tf_op jit(solution)/shard_map/ppermute | solution.py:13
Sparse Core Ops, SparseCore 0:
  9.2 29.3 all-gather.2
  40.4 86.0 all-gather.4
where the time goes:
time: 245 us; the launch traced here: 244 us
  waiting for transfers between devices  164 us (67%)
  starting transfers between devices  26.9 us (11%)
  matrix products  26.5 us (11%)
  between operations  13.6 us (6%)
  local copies, waits for them, and re-layouts  9.27 us (4%)
  other arithmetic  3.71 us (2%)
    ppermute x9, waiting for transfers between devices, shifted(): return lax.ppermute(block, axis, route)  91.7 us
    all_gather x1, waiting for transfers between devices, per_device(): lax.all_gather(off_blocks, 'rhs', axis=2, tiled=True)  41.2 us
    all_gather x1, waiting for transfers between devices, per_device(): lax.all_gather(diag_inverse, 'rhs', axis=1, tiled=True)  29.9 us
    ppermute x9, starting transfers between devices, shifted(): return lax.ppermute(block, axis, route)  26.9 us
    dot_general x4, matrix products, per_device(): jnp.einsum('irb,iab->ira', residue, full_diag, preferred_element_type=jnp...  26.5 us
    gather x3, local copies, waits for them, and re-layouts, per_device(): picked = jnp.take(window, offset, axis=0)  8.37 us
  transfers between devices with their start and end apart: 11, of which 11 were waited for; matrix products, arithmetic and copies ran while one was open for 3% of the time, Pallas kernels for 0%

commit v1 on v0

v1 whole, which is shorter than its diff:
```python
import functools

import jax
import jax.numpy as jnp
from jax import lax
from jax.experimental import pallas as pl
from jax.experimental.pallas import tpu as pltpu
from jax.sharding import PartitionSpec as P

LEVELS = 4
REACH = 4
CAP = 4
ANY = pl.BlockSpec(memory_space=pl.ANY)
SMEM = pl.BlockSpec(memory_space=pltpu.SMEM)
VMEM = pl.BlockSpec(memory_space=pltpu.VMEM)
PARAMS = pltpu.CompilerParams(vmem_limit_bytes=24 * 2**20)

PLACES = {1: range(0, 4), 2: range(1, 6), 3: range(2, 7), 0: range(4, 8)}
CHUNKS = ((0, 2), (2, 4), (4, 6), (6, 7))
FORWARD = (True, True, False, False)


def order_of(level_ref, order_ref):
    at = jnp.int32(0)
    starts = {}
    for level in (1, 2, 3, 0):
        starts[level] = at
        for row in range(8):
            here = level_ref[row] == level

            @pl.when(here)
            def _(at=at, row=row):
                order_ref[at] = jnp.int32(row)

            at = at + here.astype(jnp.int32)
    return starts


def sort_kernel(level_ref, off_ref, *refs):
    chunks, (order_ref, sems) = refs[: len(CHUNKS)], refs[len(CHUNKS) :]
    order_of(level_ref, order_ref)
    copies = []
    for chunk_ref, (low, high) in zip(chunks, CHUNKS):
        for place in range(low, high):
            copies.append(
                pltpu.make_async_copy(off_ref.at[order_ref[place]], chunk_ref.at[place - low], sems.at[place])
            )
    for copy in copies:
        copy.start()
    for copy in copies:
        copy.wait()


def sort_call(level, off):
    return pl.pallas_call(
        sort_kernel,
        out_shape=[jax.ShapeDtypeStruct((high - low,) + off.shape[1:], off.dtype) for low, high in CHUNKS],
        in_specs=[SMEM, ANY],
        out_specs=[VMEM] * len(CHUNKS),
        scratch_shapes=[pltpu.SMEM((8,), jnp.int32), pltpu.SemaphoreType.DMA((8,))],
        compiler_params=PARAMS,
    )(level, off)


TABLE = 80
TAIL = 16


def table_kernel(rows_at_ref, level_ref, columns_ref, one_ref, two_ref, three_ref, table_ref, slot_ref, levels_ref, near_ref, sem):
    parts = [
        ref[ref.shape[0] - TAIL :, :128].astype(jnp.float32).astype(jnp.int32)[:8] for ref in (one_ref, two_ref, three_ref)
    ]
    lane = lax.broadcasted_iota(jnp.int32, (8, 128), 0)
    levels_ref[...] = jnp.where(lane == 0, parts[0], jnp.where(lane == 1, parts[1], parts[2]))
    copy = pltpu.make_async_copy(levels_ref, near_ref, sem)
    copy.start()
    starts = order_of(level_ref, table_ref)
    ends = {1: starts[2], 2: starts[3], 3: starts[0], 0: jnp.int32(8)}
    for level in range(LEVELS):
        table_ref[8 + level] = starts[level]
        table_ref[12 + level] = ends[level]
    copy.wait()
    for distance in range(REACH):
        seen = [jnp.int32(0)] * LEVELS
        for row in range(8):
            level = level_ref[row] if distance == 0 else near_ref[distance - 1, row] & 3
            rank = jnp.int32(0)
            for other in range(LEVELS):
                here = level == other
                rank = jnp.where(here, seen[other], rank)
                seen[other] = seen[other] + here.astype(jnp.int32)
            slot_ref[distance * 8 + row] = 16 * jnp.minimum(level, 2) + 4 * distance + jnp.minimum(rank, CAP - 1)
    base = rows_at_ref[0]
    for place in range(7):
        row = table_ref[place]
        for k in range(8):
            column = columns_ref[row, k]
            distance = jnp.clip(base - lax.shift_right_logical(column, 3), 0, REACH - 1)
            table_ref[16 + 8 * place + k] = slot_ref[distance * 8 + (column & 7)]


def table_call(rows_at, level, columns, received):
    return pl.pallas_call(
        table_kernel,
        out_shape=jax.ShapeDtypeStruct((TABLE,), jnp.int32),
        in_specs=[SMEM] * 3 + [VMEM] * 3,
        out_specs=SMEM,
        scratch_shapes=[
            pltpu.SMEM((32,), jnp.int32),
            pltpu.VMEM((8, 128), jnp.int32),
            pltpu.SMEM((8, 128), jnp.int32),
            pltpu.SemaphoreType.DMA,
        ],
        compiler_params=PARAMS,
    )(rows_at, level, columns, *received)


def dot_t(x, y):
    return lax.dot_general(x, y, (((1,), (1,)), ((), ())), preferred_element_type=jnp.float32)


def in_order(x_at, total):
    return pltpu.roll(total, lax.rem(x_at + 3, 4) * 64, 1)


def first_kernel(x_ref, level_ref, right_ref, own_ref, before_ref, after_ref, across_ref, out_ref, solved_ref, order_ref, sems):
    x_at = x_ref[0]
    columns = right_ref.shape[1]
    begin = order_of(level_ref, order_ref)[0]

    def store(place):
        at = pl.multiple_of((place - begin) * columns, columns)
        return pltpu.make_async_copy(
            solved_ref.at[pl.ds(at, columns)], out_ref.at[order_ref[place]], sems.at[place - 4]
        )

    lane = lax.broadcasted_iota(jnp.int32, (TAIL, 256), 1)
    tail = jnp.zeros((TAIL, 256), jnp.int32)
    for row in range(8):
        tail = jnp.where(lane == row, level_ref[row], tail)
    solved_ref[CAP * columns :] = tail.astype(jnp.float32).astype(solved_ref.dtype)
    for place in PLACES[0]:

        @pl.when(place >= begin)
        def _(place=place):
            row = order_ref[place]
            inverse = jnp.concatenate([ref[row] for ref in (before_ref, own_ref, after_ref, across_ref)], axis=0)
            updated = in_order(x_at, dot_t(right_ref[row], inverse)).astype(solved_ref.dtype)
            solved_ref[pl.ds(pl.multiple_of((place - begin) * columns, columns), columns)] = updated
            store(place).start()

    for place in PLACES[0]:

        @pl.when(place >= begin)
        def _(place=place):
            store(place).wait()


def first_call(x_at, level, right, diag_pieces):
    rows, columns, size = right.shape
    return pl.pallas_call(
        first_kernel,
        out_shape=[
            jax.ShapeDtypeStruct(right.shape, right.dtype),
            jax.ShapeDtypeStruct((CAP * columns + TAIL, size), right.dtype),
        ],
        in_specs=[SMEM, SMEM] + [VMEM] * 5,
        out_specs=[ANY, VMEM],
        scratch_shapes=[pltpu.SMEM((8,), jnp.int32), pltpu.SemaphoreType.DMA((CAP,))],
        compiler_params=PARAMS,
        cost_estimate=pl.CostEstimate(flops=2 * CAP * columns * size * size, bytes_accessed=3 * 2**20, transcendentals=0),
    )(x_at, level, right, *diag_pieces)


def chunk_of(place):
    return next(n for n, (low, high) in enumerate(CHUNKS) if low <= place < high)


def level_kernel(level, used, x_ref, table_ref, right_ref, *refs):
    places = PLACES[level]
    refs = list(refs)

    def take(count):
        taken = refs[:count]
        del refs[:count]
        return taken

    diag_refs = take(4)
    parts = {n: take(5 if FORWARD[n] else 4) for n in used}
    windows = take(4 * level)
    take(1)
    out_ref = take(1)[0]
    solved_ref = take(1)[0]
    window, window_sems, out_sems = refs
    columns = right_ref.shape[1]
    x_at = x_ref[0]
    begin, end = table_ref[8 + level], table_ref[12 + level]

    def block(place, k):
        n = chunk_of(place)
        low, high = CHUNKS[n]
        at, half = place - low, (high - low) // 2
        own, before, after = (ref[at, k] for ref in parts[n][:3])
        across = parts[n][3:]
        if not FORWARD[n]:
            last = across[0][at, k]
        elif high - low == 1:
            last = across[0][0, k] if k < 4 else across[1][0, k - 4]
        else:
            last = across[0][at, k] if at < half else across[1][at - half, k]
        return jnp.concatenate([before, own, after, last], axis=0)

    def store(place):
        at = pl.multiple_of((place - begin) * columns, columns)
        return pltpu.make_async_copy(
            solved_ref.at[pl.ds(at, columns)], out_ref.at[table_ref[place]], out_sems.at[place - places[0]]
        )

    incoming = [
        pltpu.make_async_copy(
            ref.at[pl.ds(0, CAP * columns)], window.at[pl.ds(n * CAP * columns, CAP * columns)], window_sems.at[n]
        )
        for n, ref in enumerate(windows)
    ]
    for copy in incoming:
        copy.start()
    for copy in incoming:
        copy.wait()
    for place in places:

        @pl.when((place >= begin) & (place < end))
        def _(place=place):
            row = table_ref[place]
            total = jnp.zeros(right_ref.shape[1:], jnp.float32)
            for k in range(8):
                at = pl.multiple_of(table_ref[16 + 8 * place + k] * columns, columns)
                total = total + dot_t(window[pl.ds(at, columns)], block(place, k))
            residue = (right_ref[row].astype(jnp.float32) - in_order(x_at, total)).astype(jnp.bfloat16)
            own, before, after, across = (ref[row] for ref in diag_refs)
            updated = dot_t(residue, jnp.concatenate([before, own, after, across], axis=0))
            at = pl.multiple_of((place - begin) * columns, columns)
            solved_ref[pl.ds(at, columns)] = in_order(x_at, updated).astype(solved_ref.dtype)
            store(place).start()

    for place in places:

        @pl.when((place >= begin) & (place < end))
        def _(place=place):
            store(place).wait()


def level_call(level, x_at, table, right, diag_pieces, parts, windows, out):
    rows, columns, size = right.shape
    places = PLACES[level]
    used = sorted({chunk_of(place) for place in places})
    flat = [piece for n in used for piece in parts[n]]
    operands = [x_at, table, right, *diag_pieces, *flat, *windows, out]
    count = len(places)
    return pl.pallas_call(
        functools.partial(level_kernel, level, used),
        out_shape=[
            jax.ShapeDtypeStruct(out.shape, out.dtype),
            jax.ShapeDtypeStruct((CAP * columns, size), out.dtype),
        ],
        in_specs=[SMEM, SMEM] + [VMEM] * (len(operands) - 3) + [ANY],
        out_specs=[ANY, VMEM],
        input_output_aliases={len(operands) - 1: 0},
        scratch_shapes=[
            pltpu.VMEM((4 * level * CAP * columns, size), out.dtype),
            pltpu.SemaphoreType.DMA((4 * level,)),
            pltpu.SemaphoreType.DMA((count,)),
        ],
        compiler_params=PARAMS,
        cost_estimate=pl.CostEstimate(
            flops=2 * CAP * 9 * columns * size * size, bytes_accessed=8 * 2**20, transcendentals=0
        ),
    )(*operands)


def round_x(block, distance):
    size = lax.axis_size("rhs")
    return lax.ppermute(block, "rhs", [(i, (i + distance) % size) for i in range(size)])


def up(block, distance):
    size = lax.axis_size("rows")
    return lax.ppermute(block, "rows", [(i, i + distance) for i in range(size - distance)])


def per_device(right, off, diag, level, columns):
    x_at = lax.axis_index("rhs").astype(jnp.int32).reshape(1)
    rows_at = lax.axis_index("rows").astype(jnp.int32).reshape(1)
    diag_pieces = [diag, round_x(diag, 1), round_x(diag, -1), round_x(diag, 2)]
    chunks = sort_call(level, off)
    parts = []
    for chunk, forward in zip(chunks, FORWARD):
        before, after = round_x(chunk, 1), round_x(chunk, -1)
        if not forward:
            across = [round_x(chunk, 2)]
        elif chunk.shape[0] == 1:
            across = [round_x(before[:, :4], 1), round_x(after[:, 4:], -1)]
        else:
            half = chunk.shape[0] // 2
            across = [round_x(before[:half], 1), round_x(after[half:], -1)]
        parts.append([chunk, before, after, *across])
    out, solved = first_call(x_at, level, right, diag_pieces)
    windows = [solved] + [up(solved, distance) for distance in range(1, REACH)]
    table = table_call(rows_at, level, columns, windows[1:])
    for level_now in range(1, LEVELS):
        out, solved = level_call(level_now, x_at, table, right, diag_pieces, parts, windows, out)
        if level_now < LEVELS - 1:
            windows += [solved] + [up(solved, distance) for distance in range(1, REACH)]
    return out


def solution(mesh):
    return jax.shard_map(
        per_device,
        mesh=mesh,
        in_specs=(
            P("rows", "rhs", None),
            P("rows", None, "rhs", None),
            P("rows", "rhs", None),
            P("rows"),
            P("rows", None),
        ),
        out_specs=P("rows", "rhs", None),
        check_vma=False,
    )
```

time: 245 us -> 159 us (0.65)
  the two profiles are of different devices: /device:TPU:8 before, /device:TPU:62 now
where the time goes in v1:
time: 159 us; the launch traced here: 156 us
  starting transfers between devices  62.5 us (39%)
  waiting for transfers between devices  60.6 us (38%)
  Pallas kernels  20.2 us (13%)
  local copies, waits for them, and re-layouts  12.5 us (8%)
    ppermute x17, waiting for transfers between devices, round_x(): lax.ppermute(block, 'rhs', [(i, (i + distance) % size) for i in range(siz...  38.1 us
    ppermute x9, starting transfers between devices, up(): lax.ppermute(block, 'rows', [(i, i + distance) for i in range(size - dist...  33.3 us
    ppermute x17, starting transfers between devices, round_x(): lax.ppermute(block, 'rhs', [(i, (i + distance) % size) for i in range(siz...  29.3 us
    ppermute x9, waiting for transfers between devices, up(): lax.ppermute(block, 'rows', [(i, i + distance) for i in range(size - dist...  22.4 us
    pallas_call x3, Pallas kernels, level_call(): pl.pallas_call(functools.partial(level_kernel, level, used), out_shape=[j...  14.6 us
    unnamed x46, local copies, waits for them, and re-layouts  9.15 us
    slice x4, local copies, waits for them, and re-layouts, per_device(): across = [round_x(before[:half], 1), round_x(after[half:], -1)]  3.39 us
  transfers between devices with their start and end apart: 26, of which 7 were waited for; matrix products, arithmetic and copies ran while one was open for 2% of the time, Pallas kernels for 9%

profile of v1, /device:TPU:62, one launch (start us, length us, event | category | flops | bytes accessed | tf_op | source)
XLA Modules:
  0.0 156.4 jit_solution(17325241793979774065)
XLA Ops:
  0.0 0.5 collective-permute-start
  0.5 1.5 collective-permute-start.1
  2.0 1.6 %copy-done.17 = bf16[8,8,64,256]{3,2,1,0:T(8,128)(2,1)S(1)} copy-done((bf16[8,8,64,256]{3,2,1,0:T(8,128)(2,1)S(1)}, bf16[8,8,64,256]{3,2,1,0:T(8,128)(2,1)}, u32[]{:S(2)}) %copy-start.17) | copy-done | bytes 2097176
  3.6 0.7 copy-done.20
  4.3 1.8 %shard_map.57 = (bf16[2,8,64,256]{3,2,1,0:T(8,128)(2,1)}, bf16[2,8,64,256]{3,2,1,0:T(8,128)(2,1)S(1)}, bf16[2,8,64,256]{3,2,1,0:T(8,128)(2,1)}, bf16[1,8,64,256]{3,2,1,0:T(8,128)(2,1)S(1)}) custom-call(s32[8]{0:T(128)S(1)} %copy-done.20, bf16[8,8,64,256]{3,2,1,0:T(8,128)(2,1)S(1)} %copy-done.17), custom_call_target="tpu_custom_call" | custom-call | tf_op jit(solution)/shard_map/pallas_call | solution.py:55
  6.1 0.7 copy-done.18
  6.8 1.7 %collective-permute-start.6 = (bf16[2,8,64,256]{3,2,1,0:T(8,128)(2,1)S(1)}, bf16[2,8,64,256]{3,2,1,0:T(8,128)(2,1)S(1)}, u32[]{:S(2)}, u32[]{:S(2)}) collective-permute-start(bf16[2,8,64,256]{3,2,1,0:T(8,128)(2,1)S(1)} %get-tuple-element.17.refs_9_.refs_4_), channel_id=1, source_target_pairs={{0,1},{1,2},{2,3},{3,0},{4,5},{5,6},{6,7},{7,4},{8,9},{9,10},{10,1... | collective-permute-start | bytes 1572872 | tf_op jit(solution)/shard_map/ppermute | solution.py:282
  8.5 0.3 collective-permute-start.7
  8.8 2.9 %collective-permute-start.16 = (bf16[2,8,64,256]{3,2,1,0:T(8,128)(2,1)}, bf16[2,8,64,256]{3,2,1,0:T(8,128)(2,1)}, u32[]{:S(2)}, u32[]{:S(2)}) collective-permute-start(bf16[2,8,64,256]{3,2,1,0:T(8,128)(2,1)} %get-tuple-element.20.refs_4_), channel_id=1, source_target_pairs={{0,1},{1,2},{2,3},{3,0},{4,5},{5,6},{6,7},{7,4},{8,9},{9,10},{10,1... | collective-permute-start | bytes 1572872 | tf_op jit(solution)/shard_map/ppermute | solution.py:282
  11.7 0.0 collective-permute-done.before_ref.refs_1_
  11.8 0.9 collective-permute-start.17
  12.7 16.0 %collective-permute-done.2.across_ref.refs_3_ = bf16[8,64,256]{2,1,0:T(8,128)(2,1)S(1)} collective-permute-done((bf16[8,64,256]{2,1,0:T(8,128)(2,1)S(1)}, bf16[8,64,256]{2,1,0:T(8,128)(2,1)S(1)}, u32[]{:S(2)}, u32[]{:S(2)}) %collective-permute-start.2) | collective-permute-done | bytes 262176 | tf_op jit(solution)/shard_map/ppermute | solution.py:282
  28.7 1.6 shard_map.55
  30.3 1.9 %collective-permute-start.3 = (bf16[528,256]{1,0:T(8,128)(2,1)S(1)}, bf16[528,256]{1,0:T(8,128)(2,1)S(1)}, u32[]{:S(2)}, u32[]{:S(2)}) collective-permute-start(bf16[528,256]{1,0:T(8,128)(2,1)S(1)} %get-tuple-element.16.refs_14_.refs_18_.refs_17_), channel_id=1, source_target_pairs={{0,4},{4,8},{8,12},{12,16},{16,20},{20,24},{24,28},{28,32},{32,36}... | collective-permute-start | bytes 811016 | tf_op jit(solution)/shard_map/ppermute | solution.py:287
  32.3 3.8 %collective-permute-start.4 = (bf16[528,256]{1,0:T(8,128)(2,1)S(1)}, bf16[528,256]{1,0:T(8,128)(2,1)S(1)}, u32[]{:S(2)}, u32[]{:S(2)}) collective-permute-start(bf16[528,256]{1,0:T(8,128)(2,1)S(1)} %get-tuple-element.16.refs_14_.refs_18_.refs_17_), channel_id=1, source_target_pairs={{0,8},{4,12},{8,16},{12,20},{16,24},{20,28},{24,32},{28,36},{32,40... | collective-permute-start | bytes 811016 | tf_op jit(solution)/shard_map/ppermute | solution.py:287
  36.1 6.7 %collective-permute-start.5 = (bf16[528,256]{1,0:T(8,128)(2,1)S(1)}, bf16[528,256]{1,0:T(8,128)(2,1)S(1)}, u32[]{:S(2)}, u32[]{:S(2)}) collective-permute-start(bf16[528,256]{1,0:T(8,128)(2,1)S(1)} %get-tuple-element.16.refs_14_.refs_18_.refs_17_), channel_id=1, source_target_pairs={{0,12},{4,16},{8,20},{12,24},{16,28},{20,32},{24,36},{28,40},{32,4... | collective-permute-start | bytes 811016 | tf_op jit(solution)/shard_map/ppermute | solution.py:287
  42.8 10.9 %collective-permute-start.8 = (bf16[1,8,64,256]{3,2,1,0:T(8,128)(2,1)S(1)}, bf16[1,8,64,256]{3,2,1,0:T(8,128)(2,1)S(1)}, u32[]{:S(2)}, u32[]{:S(2)}) collective-permute-start(bf16[1,8,64,256]{3,2,1,0:T(8,128)(2,1)S(1)} %slice.16), channel_id=1, source_target_pairs={{0,1},{1,2},{2,3},{3,0},{4,5},{5,6},{6,7},{7,4},{8,9},{9,10},{10,1... | collective-permute-start | bytes 786440 | tf_op jit(solution)/shard_map/ppermute | solution.py:282
  53.7 0.1 collective-permute-start.9
  53.8 3.2 %collective-permute-start.10 = (bf16[2,8,64,256]{3,2,1,0:T(8,128)(2,1)}, bf16[2,8,64,256]{3,2,1,0:T(8,128)(2,1)}, u32[]{:S(2)}, u32[]{:S(2)}) collective-permute-start(bf16[2,8,64,256]{3,2,1,0:T(8,128)(2,1)} %get-tuple-element.18.refs_14_.refs_9_), channel_id=1, source_target_pairs={{0,1},{1,2},{2,3},{3,0},{4,5},{5,6},{6,7},{7,4},{8,9},{9,10},{10,1... | collective-permute-start | bytes 1572872 | tf_op jit(solution)/shard_map/ppermute | solution.py:282
  57.1 1.7 %slice.18 = bf16[1,8,64,256]{3,2,1,0:T(8,128)(2,1)} slice(bf16[2,8,64,256]{3,2,1,0:T(8,128)(2,1)} %collective-permute-done.16.refs_5_), slice={[0:1], [0:8], [0:64], [0:256]} | slice | bytes 524288 | tf_op jit(solution)/shard_map/slice | solution.py:304
  58.8 1.7 %slice.19 = bf16[1,8,64,256]{3,2,1,0:T(8,128)(2,1)} slice(bf16[2,8,64,256]{3,2,1,0:T(8,128)(2,1)} %collective-permute-done.17.refs_6_), slice={[1:2], [0:8], [0:64], [0:256]} | slice | bytes 524288 | tf_op jit(solution)/shard_map/slice | solution.py:304
  60.4 3.2 %collective-permute-start.18 = (bf16[1,8,64,256]{3,2,1,0:T(8,128)(2,1)}, bf16[1,8,64,256]{3,2,1,0:T(8,128)(2,1)}, u32[]{:S(2)}, u32[]{:S(2)}) collective-permute-start(bf16[1,8,64,256]{3,2,1,0:T(8,128)(2,1)} %slice.18), channel_id=1, source_target_pairs={{0,1},{1,2},{2,3},{3,0},{4,5},{5,6},{6,7},{7,4},{8,9},{9,10},{10,1... | collective-permute-start | bytes 786440 | tf_op jit(solution)/shard_map/ppermute | solution.py:282
  63.7 0.7 copy-done.11
  64.4 0.7 copy-done.14
  65.1 1.9 %collective-permute-start.12 = (bf16[2,8,64,256]{3,2,1,0:T(8,128)(2,1)}, bf16[2,8,64,256]{3,2,1,0:T(8,128)(2,1)}, u32[]{:S(2)}, u32[]{:S(2)}) collective-permute-start(bf16[2,8,64,256]{3,2,1,0:T(8,128)(2,1)} %get-tuple-element.18.refs_14_.refs_9_), channel_id=1, source_target_pairs={{0,2},{1,3},{2,0},{3,1},{4,6},{5,7},{6,4},{7,5},{8,10},{9,11},{10,... | collective-permute-start | bytes 1572872 | tf_op jit(solution)/shard_map/ppermute | solution.py:282
  67.0 2.3 %shard_map.56.table_ref = s32[80]{0:T(128)S(1)} custom-call(s32[1]{0:T(128)} %bitcast.1.rows_at_ref, s32[8]{0:T(128)S(1)} %copy-done.21, s32[8,8]{1,0:T(8,128)S(1)} %copy-done.22, bf16[528,256]{1,0:T(8,128)(2,1)S(1)} %collective-permute-done.3.one_ref.refs_15_.refs_19_.refs_18_, ...), custom_call_target="tpu_custom_call" | custom-call | tf_op jit(solution)/shard_map/pallas_call | solution.py:103
  69.2 18.5 %collective-permute-done.18.refs_7_ = bf16[1,8,64,256]{3,2,1,0:T(8,128)(2,1)} collective-permute-done((bf16[1,8,64,256]{3,2,1,0:T(8,128)(2,1)}, bf16[1,8,64,256]{3,2,1,0:T(8,128)(2,1)}, u32[]{:S(2)}, u32[]{:S(2)}) %collective-permute-start.18) | collective-permute-done | bytes 262176 | tf_op jit(solution)/shard_map/ppermute | solution.py:282
  87.8 3.5 %collective-permute-done.19.refs_8_ = bf16[1,8,64,256]{3,2,1,0:T(8,128)(2,1)} collective-permute-done((bf16[1,8,64,256]{3,2,1,0:T(8,128)(2,1)}, bf16[1,8,64,256]{3,2,1,0:T(8,128)(2,1)}, u32[]{:S(2)}, u32[]{:S(2)}) %collective-permute-start.19) | collective-permute-done | bytes 262176 | tf_op jit(solution)/shard_map/ppermute | solution.py:282
  91.3 0.9 copy-done.3
  92.2 0.9 copy-done.6
  93.2 1.0 copy-done.9
  94.1 0.9 copy-done.12
  95.1 0.9 copy-done.15
  96.0 4.2 %shard_map.58 = (bf16[8,128,256]{2,1,0:T(8,128)(2,1)}, bf16[512,256]{1,0:T(8,128)(2,1)S(1)}) custom-call(s32[1]{0:T(128)} %bitcast.x_ref, s32[80]{0:T(128)S(1)} %shard_map.56.table_ref, bf16[8,128,256]{2,1,0:T(8,128)(2,1)S(1)} %copy-done, bf16[8,64,256]{2,1,0:T(8,128)(2,1)S(1)} %copy-done.1, ...), custom_call_target="tpu_custom_call", output_to_operand_aliasing={{0}: (21, {})} | custom-call | flops 603979776 | bytes 8388608 | tf_op jit(solution)/shard_map/pallas_call | solution.py:259
  100.2 1.9 %collective-permute-start.20 = (bf16[512,256]{1,0:T(8,128)(2,1)S(1)}, bf16[512,256]{1,0:T(8,128)(2,1)S(1)}, u32[]{:S(2)}, u32[]{:S(2)}) collective-permute-start(bf16[512,256]{1,0:T(8,128)(2,1)S(1)} %get-tuple-element.22.refs_22_.refs_21_), channel_id=1, source_target_pairs={{0,4},{4,8},{8,12},{12,16},{16,20},{20,24},{24,28},{28,32},{32,36}... | collective-permute-start | bytes 786440 | tf_op jit(solution)/shard_map/ppermute | solution.py:287
  102.1 1.9 %collective-permute-start.21 = (bf16[512,256]{1,0:T(8,128)(2,1)S(1)}, bf16[512,256]{1,0:T(8,128)(2,1)S(1)}, u32[]{:S(2)}, u32[]{:S(2)}) collective-permute-start(bf16[512,256]{1,0:T(8,128)(2,1)S(1)} %get-tuple-element.22.refs_22_.refs_21_), channel_id=1, source_target_pairs={{0,8},{4,12},{8,16},{12,20},{16,24},{20,28},{24,32},{28,36},{32,40... | collective-permute-start | bytes 786440 | tf_op jit(solution)/shard_map/ppermute | solution.py:287
  104.1 5.2 %collective-permute-start.22 = (bf16[512,256]{1,0:T(8,128)(2,1)S(1)}, bf16[512,256]{1,0:T(8,128)(2,1)S(1)}, u32[]{:S(2)}, u32[]{:S(2)}) collective-permute-start(bf16[512,256]{1,0:T(8,128)(2,1)S(1)} %get-tuple-element.22.refs_22_.refs_21_), channel_id=1, source_target_pairs={{0,12},{4,16},{8,20},{12,24},{16,28},{20,32},{24,36},{28,40},{32,4... | collective-permute-start | bytes 786440 | tf_op jit(solution)/shard_map/ppermute | solution.py:287
  109.3 0.3 collective-permute-start.13
  109.6 1.8 %collective-permute-start.14 = (bf16[1,8,64,256]{3,2,1,0:T(8,128)(2,1)S(1)}, bf16[1,8,64,256]{3,2,1,0:T(8,128)(2,1)S(1)}, u32[]{:S(2)}, u32[]{:S(2)}) collective-permute-start(bf16[1,8,64,256]{3,2,1,0:T(8,128)(2,1)S(1)} %copy-done.19), channel_id=1, source_target_pairs={{0,3},{1,0},{2,1},{3,2},{4,7},{5,4},{6,5},{7,6},{8,11},{9,8},{10,9... | collective-permute-start | bytes 786440 | tf_op jit(solution)/shard_map/ppermute | solution.py:282
  111.5 1.8 %collective-permute-done.21.refs_24_.refs_23_ = bf16[512,256]{1,0:T(8,128)(2,1)S(1)} collective-permute-done((bf16[512,256]{1,0:T(8,128)(2,1)S(1)}, bf16[512,256]{1,0:T(8,128)(2,1)S(1)}, u32[]{:S(2)}, u32[]{:S(2)}) %collective-permute-start.21) | collective-permute-done | bytes 262176 | tf_op jit(solution)/shard_map/ppermute | solution.py:287
  113.3 8.4 %collective-permute-done.22.refs_25_.refs_24_ = bf16[512,256]{1,0:T(8,128)(2,1)S(1)} collective-permute-done((bf16[512,256]{1,0:T(8,128)(2,1)S(1)}, bf16[512,256]{1,0:T(8,128)(2,1)S(1)}, u32[]{:S(2)}, u32[]{:S(2)}) %collective-permute-start.22) | collective-permute-done | bytes 262176 | tf_op jit(solution)/shard_map/ppermute | solution.py:287
  121.7 4.0 %shard_map.59 = (bf16[8,128,256]{2,1,0:T(8,128)(2,1)}, bf16[512,256]{1,0:T(8,128)(2,1)S(1)}) custom-call(s32[1]{0:T(128)} %bitcast.x_ref, s32[80]{0:T(128)S(1)} %shard_map.56.table_ref, bf16[8,128,256]{2,1,0:T(8,128)(2,1)S(1)} %copy-done, bf16[8,64,256]{2,1,0:T(8,128)(2,1)S(1)} %copy-done.1, ...), custom_call_target="tpu_custom_call", output_to_operand_aliasing={{0}: (29, {})} | custom-call | flops 603979776 | bytes 8388608 | tf_op jit(solution)/shard_map/pallas_call | solution.py:259
  125.6 1.9 %collective-permute-start.23 = (bf16[512,256]{1,0:T(8,128)(2,1)S(1)}, bf16[512,256]{1,0:T(8,128)(2,1)S(1)}, u32[]{:S(2)}, u32[]{:S(2)}) collective-permute-start(bf16[512,256]{1,0:T(8,128)(2,1)S(1)} %get-tuple-element.24.refs_25_), channel_id=1, source_target_pairs={{0,4},{4,8},{8,12},{12,16},{16,20},{20,24},{24,28},{28,32},{32,36}... | collective-permute-start | bytes 786440 | tf_op jit(solution)/shard_map/ppermute | solution.py:287
  127.6 5.5 %collective-permute-start.24 = (bf16[512,256]{1,0:T(8,128)(2,1)S(1)}, bf16[512,256]{1,0:T(8,128)(2,1)S(1)}, u32[]{:S(2)}, u32[]{:S(2)}) collective-permute-start(bf16[512,256]{1,0:T(8,128)(2,1)S(1)} %get-tuple-element.24.refs_25_), channel_id=1, source_target_pairs={{0,8},{4,12},{8,16},{12,20},{16,24},{20,28},{24,32},{28,36},{32,40... | collective-permute-start | bytes 786440 | tf_op jit(solution)/shard_map/ppermute | solution.py:287
  133.1 4.3 %collective-permute-start.25 = (bf16[512,256]{1,0:T(8,128)(2,1)S(1)}, bf16[512,256]{1,0:T(8,128)(2,1)S(1)}, u32[]{:S(2)}, u32[]{:S(2)}) collective-permute-start(bf16[512,256]{1,0:T(8,128)(2,1)S(1)} %get-tuple-element.24.refs_25_), channel_id=1, source_target_pairs={{0,12},{4,16},{8,20},{12,24},{16,28},{20,32},{24,36},{28,40},{32,4... | collective-permute-start | bytes 786440 | tf_op jit(solution)/shard_map/ppermute | solution.py:287
  137.5 3.2 %collective-permute-done.24.refs_27_ = bf16[512,256]{1,0:T(8,128)(2,1)S(1)} collective-permute-done((bf16[512,256]{1,0:T(8,128)(2,1)S(1)}, bf16[512,256]{1,0:T(8,128)(2,1)S(1)}, u32[]{:S(2)}, u32[]{:S(2)}) %collective-permute-start.24) | collective-permute-done | bytes 262176 | tf_op jit(solution)/shard_map/ppermute | solution.py:287
  140.7 9.0 %collective-permute-done.25.refs_28_ = bf16[512,256]{1,0:T(8,128)(2,1)S(1)} collective-permute-done((bf16[512,256]{1,0:T(8,128)(2,1)S(1)}, bf16[512,256]{1,0:T(8,128)(2,1)S(1)}, u32[]{:S(2)}, u32[]{:S(2)}) %collective-permute-start.25) | collective-permute-done | bytes 262176 | tf_op jit(solution)/shard_map/ppermute | solution.py:287
  149.7 6.5 %shard_map.60 = (bf16[8,128,256]{2,1,0:T(8,128)(2,1)}, bf16[512,256]{1,0:T(8,128)(2,1)}) custom-call(s32[1]{0:T(128)} %bitcast.x_ref, s32[80]{0:T(128)S(1)} %shard_map.56.table_ref, bf16[8,128,256]{2,1,0:T(8,128)(2,1)S(1)} %copy-done, bf16[8,64,256]{2,1,0:T(8,128)(2,1)S(1)} %copy-done.1, ...), custom_call_target="tpu_custom_call", output_to_operand_aliasing={{0}: (32, {})} | custom-call | flops 603979776 | bytes 8388608 | tf_op jit(solution)/shard_map/pallas_call | solution.py:259
  (60 shorter events, 0.2 us)
Async XLA Ops:
  0.0 11.7 %copy-start.1 = (bf16[8,64,256]{2,1,0:T(8,128)(2,1)S(1)}, bf16[8,64,256]{2,1,0:T(8,128)(2,1)}, u32[]{:S(2)}) copy-start(bf16[8,64,256]{2,1,0:T(8,128)(2,1)} %refs_0_.5) | copy-start | bytes 786436
  0.0 28.7 %copy-start = (bf16[8,128,256]{2,1,0:T(8,128)(2,1)S(1)}, bf16[8,128,256]{2,1,0:T(8,128)(2,1)}, u32[]{:S(2)}) copy-start(bf16[8,128,256]{2,1,0:T(8,128)(2,1)} %right_ref.7) | copy-start | bytes 1572868
  0.0 11.7 %collective-permute-start = (bf16[8,64,256]{2,1,0:T(8,128)(2,1)}, bf16[8,64,256]{2,1,0:T(8,128)(2,1)S(1)}, u32[]{:S(2)}, u32[]{:S(2)}) collective-permute-start(bf16[8,64,256]{2,1,0:T(8,128)(2,1)} %refs_0_.5), channel_id=1, source_target_pairs={{0,1},{1,2},{2,3},{3,0},{4,5},{5,6},{6,7},{7,4},{8,9},{9,10},{10,1... | collective-permute-start | bytes 786440 | tf_op jit(solution)/shard_map/ppermute | solution.py:282
  0.5 11.3 %collective-permute-start.1 = (bf16[8,64,256]{2,1,0:T(8,128)(2,1)}, bf16[8,64,256]{2,1,0:T(8,128)(2,1)S(1)}, u32[]{:S(2)}, u32[]{:S(2)}) collective-permute-start(bf16[8,64,256]{2,1,0:T(8,128)(2,1)} %refs_0_.5), channel_id=1, source_target_pairs={{0,3},{1,0},{2,1},{3,2},{4,7},{5,4},{6,5},{7,6},{8,11},{9,8},{10,9... | collective-permute-start | bytes 786440 | tf_op jit(solution)/shard_map/ppermute | solution.py:282
  2.0 1.6 %copy-start.17 = (bf16[8,8,64,256]{3,2,1,0:T(8,128)(2,1)S(1)}, bf16[8,8,64,256]{3,2,1,0:T(8,128)(2,1)}, u32[]{:S(2)}) copy-start(bf16[8,8,64,256]{3,2,1,0:T(8,128)(2,1)} %off_ref.1) | copy-start | bytes 6291460
  4.3 24.5 %copy-start.21 = (s32[8]{0:T(128)S(1)}, s32[8]{0:T(128)}, u32[]{:S(2)}) copy-start(s32[8]{0:T(128)} %level_ref.5) | copy-start | bytes 100
  6.1 0.7 copy-start.18
  6.8 60.1 %copy-start.22 = (s32[8,8]{1,0:T(8,128)S(1)}, s32[8,8]{1,0:T(8,128)}, u32[]{:S(2)}) copy-start(s32[8,8]{1,0:T(8,128)} %columns_ref.1) | copy-start | bytes 772
  6.8 25.5 %collective-permute-start.6 = (bf16[2,8,64,256]{3,2,1,0:T(8,128)(2,1)S(1)}, bf16[2,8,64,256]{3,2,1,0:T(8,128)(2,1)S(1)}, u32[]{:S(2)}, u32[]{:S(2)}) collective-permute-start(bf16[2,8,64,256]{3,2,1,0:T(8,128)(2,1)S(1)} %get-tuple-element.17.refs_9_.refs_4_), channel_id=1, source_target_pairs={{0,1},{1,2},{2,3},{3,0},{4,5},{5,6},{6,7},{7,4},{8,9},{9,10},{10,1... | collective-permute-start | bytes 1572872 | tf_op jit(solution)/shard_map/ppermute | solution.py:282
  8.5 27.6 %collective-permute-start.7 = (bf16[2,8,64,256]{3,2,1,0:T(8,128)(2,1)S(1)}, bf16[2,8,64,256]{3,2,1,0:T(8,128)(2,1)S(1)}, u32[]{:S(2)}, u32[]{:S(2)}) collective-permute-start(bf16[2,8,64,256]{3,2,1,0:T(8,128)(2,1)S(1)} %get-tuple-element.17.refs_9_.refs_4_), channel_id=1, source_target_pairs={{0,3},{1,0},{2,1},{3,2},{4,7},{5,4},{6,5},{7,6},{8,11},{9,8},{10,9... | collective-permute-start | bytes 1572872 | tf_op jit(solution)/shard_map/ppermute | solution.py:282
  8.8 34.0 %collective-permute-start.16 = (bf16[2,8,64,256]{3,2,1,0:T(8,128)(2,1)}, bf16[2,8,64,256]{3,2,1,0:T(8,128)(2,1)}, u32[]{:S(2)}, u32[]{:S(2)}) collective-permute-start(bf16[2,8,64,256]{3,2,1,0:T(8,128)(2,1)} %get-tuple-element.20.refs_4_), channel_id=1, source_target_pairs={{0,1},{1,2},{2,3},{3,0},{4,5},{5,6},{6,7},{7,4},{8,9},{9,10},{10,1... | collective-permute-start | bytes 1572872 | tf_op jit(solution)/shard_map/ppermute | solution.py:282
  11.7 17.0 %collective-permute-start.2 = (bf16[8,64,256]{2,1,0:T(8,128)(2,1)S(1)}, bf16[8,64,256]{2,1,0:T(8,128)(2,1)S(1)}, u32[]{:S(2)}, u32[]{:S(2)}) collective-permute-start(bf16[8,64,256]{2,1,0:T(8,128)(2,1)S(1)} %copy-done.1), channel_id=1, source_target_pairs={{0,2},{1,3},{2,0},{3,1},{4,6},{5,7},{6,4},{7,5},{8,10},{9,11},{10,... | collective-permute-start | bytes 786440 | tf_op jit(solution)/shard_map/ppermute | solution.py:282
  11.8 18.6 %copy-start.2 = (bf16[8,64,256]{2,1,0:T(8,128)(2,1)}, bf16[8,64,256]{2,1,0:T(8,128)(2,1)S(1)}, u32[]{:S(2)}) copy-start(bf16[8,64,256]{2,1,0:T(8,128)(2,1)S(1)} %collective-permute-done.1.after_ref.refs_2_) | copy-start | bytes 786436
  11.8 42.0 %collective-permute-start.17 = (bf16[2,8,64,256]{3,2,1,0:T(8,128)(2,1)}, bf16[2,8,64,256]{3,2,1,0:T(8,128)(2,1)}, u32[]{:S(2)}, u32[]{:S(2)}) collective-permute-start(bf16[2,8,64,256]{3,2,1,0:T(8,128)(2,1)} %get-tuple-element.20.refs_4_), channel_id=1, source_target_pairs={{0,3},{1,0},{2,1},{3,2},{4,7},{5,4},{6,5},{7,6},{8,11},{9,8},{10,9... | collective-permute-start | bytes 1572872 | tf_op jit(solution)/shard_map/ppermute | solution.py:282
  28.7 1.6 %copy-start.5 = (bf16[8,64,256]{2,1,0:T(8,128)(2,1)}, bf16[8,64,256]{2,1,0:T(8,128)(2,1)S(1)}, u32[]{:S(2)}) copy-start(bf16[8,64,256]{2,1,0:T(8,128)(2,1)S(1)} %collective-permute-done.2.across_ref.refs_3_) | copy-start | bytes 786436
  30.3 30.1 %copy-start.8 = (bf16[528,256]{1,0:T(8,128)(2,1)}, bf16[528,256]{1,0:T(8,128)(2,1)S(1)}, u32[]{:S(2)}) copy-start(bf16[528,256]{1,0:T(8,128)(2,1)S(1)} %get-tuple-element.16.refs_14_.refs_18_.refs_17_) | copy-start | bytes 811012
  30.3 23.5 %collective-permute-start.3 = (bf16[528,256]{1,0:T(8,128)(2,1)S(1)}, bf16[528,256]{1,0:T(8,128)(2,1)S(1)}, u32[]{:S(2)}, u32[]{:S(2)}) collective-permute-start(bf16[528,256]{1,0:T(8,128)(2,1)S(1)} %get-tuple-element.16.refs_14_.refs_18_.refs_17_), channel_id=1, source_target_pairs={{0,4},{4,8},{8,12},{12,16},{16,20},{20,24},{24,28},{28,32},{32,36}... | collective-permute-start | bytes 811016 | tf_op jit(solution)/shard_map/ppermute | solution.py:287
  32.3 24.8 %collective-permute-start.4 = (bf16[528,256]{1,0:T(8,128)(2,1)S(1)}, bf16[528,256]{1,0:T(8,128)(2,1)S(1)}, u32[]{:S(2)}, u32[]{:S(2)}) collective-permute-start(bf16[528,256]{1,0:T(8,128)(2,1)S(1)} %get-tuple-element.16.refs_14_.refs_18_.refs_17_), channel_id=1, source_target_pairs={{0,8},{4,12},{8,16},{12,20},{16,24},{20,28},{24,32},{28,36},{32,40... | collective-permute-start | bytes 811016 | tf_op jit(solution)/shard_map/ppermute | solution.py:287
  36.1 24.3 %collective-permute-start.5 = (bf16[528,256]{1,0:T(8,128)(2,1)S(1)}, bf16[528,256]{1,0:T(8,128)(2,1)S(1)}, u32[]{:S(2)}, u32[]{:S(2)}) collective-permute-start(bf16[528,256]{1,0:T(8,128)(2,1)S(1)} %get-tuple-element.16.refs_14_.refs_18_.refs_17_), channel_id=1, source_target_pairs={{0,12},{4,16},{8,20},{12,24},{16,28},{20,32},{24,36},{28,40},{32,4... | collective-permute-start | bytes 811016 | tf_op jit(solution)/shard_map/ppermute | solution.py:287
  42.8 20.8 %collective-permute-start.8 = (bf16[1,8,64,256]{3,2,1,0:T(8,128)(2,1)S(1)}, bf16[1,8,64,256]{3,2,1,0:T(8,128)(2,1)S(1)}, u32[]{:S(2)}, u32[]{:S(2)}) collective-permute-start(bf16[1,8,64,256]{3,2,1,0:T(8,128)(2,1)S(1)} %slice.16), channel_id=1, source_target_pairs={{0,1},{1,2},{2,3},{3,0},{4,5},{5,6},{6,7},{7,4},{8,9},{9,10},{10,1... | collective-permute-start | bytes 786440 | tf_op jit(solution)/shard_map/ppermute | solution.py:282
  53.7 10.6 %collective-permute-start.9 = (bf16[1,8,64,256]{3,2,1,0:T(8,128)(2,1)S(1)}, bf16[1,8,64,256]{3,2,1,0:T(8,128)(2,1)S(1)}, u32[]{:S(2)}, u32[]{:S(2)}) collective-permute-start(bf16[1,8,64,256]{3,2,1,0:T(8,128)(2,1)S(1)} %slice.17), channel_id=1, source_target_pairs={{0,3},{1,0},{2,1},{3,2},{4,7},{5,4},{6,5},{7,6},{8,11},{9,8},{10,9... | collective-permute-start | bytes 786440 | tf_op jit(solution)/shard_map/ppermute | solution.py:282
  53.8 50.2 %collective-permute-start.10 = (bf16[2,8,64,256]{3,2,1,0:T(8,128)(2,1)}, bf16[2,8,64,256]{3,2,1,0:T(8,128)(2,1)}, u32[]{:S(2)}, u32[]{:S(2)}) collective-permute-start(bf16[2,8,64,256]{3,2,1,0:T(8,128)(2,1)} %get-tuple-element.18.refs_14_.refs_9_), channel_id=1, source_target_pairs={{0,1},{1,2},{2,3},{3,0},{4,5},{5,6},{6,7},{7,4},{8,9},{9,10},{10,1... | collective-permute-start | bytes 1572872 | tf_op jit(solution)/shard_map/ppermute | solution.py:282
  57.1 52.3 %collective-permute-start.11 = (bf16[2,8,64,256]{3,2,1,0:T(8,128)(2,1)}, bf16[2,8,64,256]{3,2,1,0:T(8,128)(2,1)}, u32[]{:S(2)}, u32[]{:S(2)}) collective-permute-start(bf16[2,8,64,256]{3,2,1,0:T(8,128)(2,1)} %get-tuple-element.18.refs_14_.refs_9_), channel_id=1, source_target_pairs={{0,3},{1,0},{2,1},{3,2},{4,7},{5,4},{6,5},{7,6},{8,11},{9,8},{10,9... | collective-permute-start | bytes 1572872 | tf_op jit(solution)/shard_map/ppermute | solution.py:282
  60.4 27.3 %collective-permute-start.18 = (bf16[1,8,64,256]{3,2,1,0:T(8,128)(2,1)}, bf16[1,8,64,256]{3,2,1,0:T(8,128)(2,1)}, u32[]{:S(2)}, u32[]{:S(2)}) collective-permute-start(bf16[1,8,64,256]{3,2,1,0:T(8,128)(2,1)} %slice.18), channel_id=1, source_target_pairs={{0,1},{1,2},{2,3},{3,0},{4,5},{5,6},{6,7},{7,4},{8,9},{9,10},{10,1... | collective-permute-start | bytes 786440 | tf_op jit(solution)/shard_map/ppermute | solution.py:282
  63.7 0.7 copy-start.11
  64.4 26.9 %collective-permute-start.19 = (bf16[1,8,64,256]{3,2,1,0:T(8,128)(2,1)}, bf16[1,8,64,256]{3,2,1,0:T(8,128)(2,1)}, u32[]{:S(2)}, u32[]{:S(2)}) collective-permute-start(bf16[1,8,64,256]{3,2,1,0:T(8,128)(2,1)} %slice.19), channel_id=1, source_target_pairs={{0,3},{1,0},{2,1},{3,2},{4,7},{5,4},{6,5},{7,6},{8,11},{9,8},{10,9... | collective-permute-start | bytes 786440 | tf_op jit(solution)/shard_map/ppermute | solution.py:282
  64.4 0.7 copy-start.14
  65.1 44.5 %collective-permute-start.12 = (bf16[2,8,64,256]{3,2,1,0:T(8,128)(2,1)}, bf16[2,8,64,256]{3,2,1,0:T(8,128)(2,1)}, u32[]{:S(2)}, u32[]{:S(2)}) collective-permute-start(bf16[2,8,64,256]{3,2,1,0:T(8,128)(2,1)} %get-tuple-element.18.refs_14_.refs_9_), channel_id=1, source_target_pairs={{0,2},{1,3},{2,0},{3,1},{4,6},{5,7},{6,4},{7,5},{8,10},{9,11},{10,... | collective-permute-start | bytes 1572872 | tf_op jit(solution)/shard_map/ppermute | solution.py:282
  91.3 1.0 copy-start.3
  92.2 0.9 copy-start.6
  93.2 1.0 copy-start.9
  94.1 0.9 copy-start.12
  95.1 0.9 copy-start.15
  96.0 13.3 %copy-start.19 = (bf16[1,8,64,256]{3,2,1,0:T(8,128)(2,1)S(1)}, bf16[1,8,64,256]{3,2,1,0:T(8,128)(2,1)}, u32[]{:S(2)}) copy-start(bf16[1,8,64,256]{3,2,1,0:T(8,128)(2,1)} %copy-done.18) | copy-start | bytes 786436
  96.0 25.6 %copy-start.10 = (bf16[528,256]{1,0:T(8,128)(2,1)S(1)}, bf16[528,256]{1,0:T(8,128)(2,1)}, u32[]{:S(2)}) copy-start(bf16[528,256]{1,0:T(8,128)(2,1)} %copy-done.8) | copy-start | bytes 811012
  96.0 25.6 %copy-start.13 = (bf16[1,8,64,256]{3,2,1,0:T(8,128)(2,1)S(1)}, bf16[1,8,64,256]{3,2,1,0:T(8,128)(2,1)}, u32[]{:S(2)}) copy-start(bf16[1,8,64,256]{3,2,1,0:T(8,128)(2,1)} %copy-done.11) | copy-start | bytes 786436
  100.2 11.2 %collective-permute-start.20 = (bf16[512,256]{1,0:T(8,128)(2,1)S(1)}, bf16[512,256]{1,0:T(8,128)(2,1)S(1)}, u32[]{:S(2)}, u32[]{:S(2)}) collective-permute-start(bf16[512,256]{1,0:T(8,128)(2,1)S(1)} %get-tuple-element.22.refs_22_.refs_21_), channel_id=1, source_target_pairs={{0,4},{4,8},{8,12},{12,16},{16,20},{20,24},{24,28},{28,32},{32,36}... | collective-permute-start | bytes 786440 | tf_op jit(solution)/shard_map/ppermute | solution.py:287
  102.1 11.1 %collective-permute-start.21 = (bf16[512,256]{1,0:T(8,128)(2,1)S(1)}, bf16[512,256]{1,0:T(8,128)(2,1)S(1)}, u32[]{:S(2)}, u32[]{:S(2)}) collective-permute-start(bf16[512,256]{1,0:T(8,128)(2,1)S(1)} %get-tuple-element.22.refs_22_.refs_21_), channel_id=1, source_target_pairs={{0,8},{4,12},{8,16},{12,20},{16,24},{20,28},{24,32},{28,36},{32,40... | collective-permute-start | bytes 786440 | tf_op jit(solution)/shard_map/ppermute | solution.py:287
  104.1 17.6 %collective-permute-start.22 = (bf16[512,256]{1,0:T(8,128)(2,1)S(1)}, bf16[512,256]{1,0:T(8,128)(2,1)S(1)}, u32[]{:S(2)}, u32[]{:S(2)}) collective-permute-start(bf16[512,256]{1,0:T(8,128)(2,1)S(1)} %get-tuple-element.22.refs_22_.refs_21_), channel_id=1, source_target_pairs={{0,12},{4,16},{8,20},{12,24},{16,28},{20,32},{24,36},{28,40},{32,4... | collective-permute-start | bytes 786440 | tf_op jit(solution)/shard_map/ppermute | solution.py:287
  109.3 23.8 %collective-permute-start.13 = (bf16[1,8,64,256]{3,2,1,0:T(8,128)(2,1)S(1)}, bf16[1,8,64,256]{3,2,1,0:T(8,128)(2,1)S(1)}, u32[]{:S(2)}, u32[]{:S(2)}) collective-permute-start(bf16[1,8,64,256]{3,2,1,0:T(8,128)(2,1)S(1)} %copy-done.19), channel_id=1, source_target_pairs={{0,1},{1,2},{2,3},{3,0},{4,5},{5,6},{6,7},{7,4},{8,9},{9,10},{10,1... | collective-permute-start | bytes 786440 | tf_op jit(solution)/shard_map/ppermute | solution.py:282
  109.6 27.8 %collective-permute-start.14 = (bf16[1,8,64,256]{3,2,1,0:T(8,128)(2,1)S(1)}, bf16[1,8,64,256]{3,2,1,0:T(8,128)(2,1)S(1)}, u32[]{:S(2)}, u32[]{:S(2)}) collective-permute-start(bf16[1,8,64,256]{3,2,1,0:T(8,128)(2,1)S(1)} %copy-done.19), channel_id=1, source_target_pairs={{0,3},{1,0},{2,1},{3,2},{4,7},{5,4},{6,5},{7,6},{8,11},{9,8},{10,9... | collective-permute-start | bytes 786440 | tf_op jit(solution)/shard_map/ppermute | solution.py:282
  111.5 26.0 %collective-permute-start.15 = (bf16[1,8,64,256]{3,2,1,0:T(8,128)(2,1)S(1)}, bf16[1,8,64,256]{3,2,1,0:T(8,128)(2,1)S(1)}, u32[]{:S(2)}, u32[]{:S(2)}) collective-permute-start(bf16[1,8,64,256]{3,2,1,0:T(8,128)(2,1)S(1)} %copy-done.19), channel_id=1, source_target_pairs={{0,2},{1,3},{2,0},{3,1},{4,6},{5,7},{6,4},{7,5},{8,10},{9,11},{10,... | collective-permute-start | bytes 786440 | tf_op jit(solution)/shard_map/ppermute | solution.py:282
  121.6 28.1 %copy-start.4 = (bf16[8,64,256]{2,1,0:T(8,128)(2,1)S(1)}, bf16[8,64,256]{2,1,0:T(8,128)(2,1)}, u32[]{:S(2)}) copy-start(bf16[8,64,256]{2,1,0:T(8,128)(2,1)} %copy-done.2) | copy-start | bytes 786436
  121.6 28.1 %copy-start.7 = (bf16[8,64,256]{2,1,0:T(8,128)(2,1)S(1)}, bf16[8,64,256]{2,1,0:T(8,128)(2,1)}, u32[]{:S(2)}) copy-start(bf16[8,64,256]{2,1,0:T(8,128)(2,1)} %copy-done.5) | copy-start | bytes 786436
  121.6 28.1 %copy-start.16 = (bf16[1,8,64,256]{3,2,1,0:T(8,128)(2,1)S(1)}, bf16[1,8,64,256]{3,2,1,0:T(8,128)(2,1)}, u32[]{:S(2)}) copy-start(bf16[1,8,64,256]{3,2,1,0:T(8,128)(2,1)} %copy-done.14) | copy-start | bytes 786436
  125.6 11.8 %collective-permute-start.23 = (bf16[512,256]{1,0:T(8,128)(2,1)S(1)}, bf16[512,256]{1,0:T(8,128)(2,1)S(1)}, u32[]{:S(2)}, u32[]{:S(2)}) collective-permute-start(bf16[512,256]{1,0:T(8,128)(2,1)S(1)} %get-tuple-element.24.refs_25_), channel_id=1, source_target_pairs={{0,4},{4,8},{8,12},{12,16},{16,20},{20,24},{24,28},{28,32},{32,36}... | collective-permute-start | bytes 786440 | tf_op jit(solution)/shard_map/ppermute | solution.py:287
  127.6 13.1 %collective-permute-start.24 = (bf16[512,256]{1,0:T(8,128)(2,1)S(1)}, bf16[512,256]{1,0:T(8,128)(2,1)S(1)}, u32[]{:S(2)}, u32[]{:S(2)}) collective-permute-start(bf16[512,256]{1,0:T(8,128)(2,1)S(1)} %get-tuple-element.24.refs_25_), channel_id=1, source_target_pairs={{0,8},{4,12},{8,16},{12,20},{16,24},{20,28},{24,32},{28,36},{32,40... | collective-permute-start | bytes 786440 | tf_op jit(solution)/shard_map/ppermute | solution.py:287
  133.1 16.6 %collective-permute-start.25 = (bf16[512,256]{1,0:T(8,128)(2,1)S(1)}, bf16[512,256]{1,0:T(8,128)(2,1)S(1)}, u32[]{:S(2)}, u32[]{:S(2)}) collective-permute-start(bf16[512,256]{1,0:T(8,128)(2,1)S(1)} %get-tuple-element.24.refs_25_), channel_id=1, source_target_pairs={{0,12},{4,16},{8,20},{12,24},{16,28},{20,32},{24,36},{28,40},{32,4... | collective-permute-start | bytes 786440 | tf_op jit(solution)/shard_map/ppermute | solution.py:287
  (1 other events, 0.7 us)
